TPU v7x, 1024 devices: a whole 4x8x16 slice. The times are simulated.
1024 devices in a mesh: rep: 8 (over y), outer: 16 (over z), inner: 8 (over x, core).
Axes of the slice: x: 4, y: 8, z: 16, core: 2. Of those that a mesh axis runs over, the one named last changes fastest.
Arguments:
- tokens: bfloat16 [16384, 1024], P(('outer', 'inner')), may hold values from -6 to 6
- cotangent: bfloat16 [16384, 1024], P(('outer', 'inner')), may hold values from -6 to 6
- routes: int32 [16384, 8], P(('outer', 'inner'), 'rep'), may hold values from 0 to 127, as said below
- gate_weights: float32 [16384, 8], P(('outer', 'inner'), 'rep'), may hold values from 0.05 to 0.5
- w_gate: bfloat16 [128, 1024, 384], P(('outer', 'inner')), may hold values from -0.1875 to 0.1875
- w_up: bfloat16 [128, 1024, 384], P(('outer', 'inner')), may hold values from -0.1875 to 0.1875
- w_down: bfloat16 [128, 384, 1024], P(('outer', 'inner')), may hold values from -0.3125 to 0.3125
Outputs:
- combined: bfloat16 [16384, 1024], P(('outer', 'inner'), 'rep')
- grad_tokens: bfloat16 [16384, 1024], P(('outer', 'inner'), 'rep')
- grad_w_gate: bfloat16 [128, 1024, 384], P(('outer', 'inner'), 'rep')
- grad_w_up: bfloat16 [128, 1024, 384], P(('outer', 'inner'), 'rep')
- grad_w_down: bfloat16 [128, 384, 1024], P(('outer', 'inner'), 'rep')
Inputs may be any that keep to these rules, and one draw needn't show every extreme that they name: `routes`: each row names 8 different experts. The columns fall into 8 groups of 1 column; within one group and one aligned block of 128 rows no expert is named more than 2 times, and in every block and group some expert is named exactly 2 times.
All inputs are finite; a program needn't handle non-finite values.
Results may differ from a plain program's by a relative error of at most 0.019.
Values may be sent and summed in bfloat16 or wider, within the bound.
A program may use at most 32 MiB of HBM per device.

v0:
```python
import jax
import jax.numpy as jnp
from jax import lax
from jax.sharding import PartitionSpec as P


def send_rows(arrays_in):
    return (
        lax.all_to_all(
            lax.all_to_all(arrays_in[0], "outer", split_axis=0, concat_axis=0, tiled=True),
            "inner",
            split_axis=1,
            concat_axis=1,
            tiled=True,
        ),
        lax.all_to_all(
            lax.all_to_all(arrays_in[1], "outer", split_axis=0, concat_axis=0, tiled=True),
            "inner",
            split_axis=1,
            concat_axis=1,
            tiled=True,
        ),
    )


def return_rows(arrays_in):
    return lax.all_to_all(
        lax.all_to_all(arrays_in, "outer", split_axis=0, concat_axis=0, tiled=True),
        "inner",
        split_axis=1,
        concat_axis=1,
        tiled=True,
    )


def expert_forward(tok_in, w_gate, w_up, w_down):
    gate_pre = jnp.einsum("abecd,edf->abecf", tok_in, w_gate, preferred_element_type=jnp.float32)
    up_pre = jnp.einsum("abecd,edf->abecf", tok_in, w_up, preferred_element_type=jnp.float32)
    sigmoid_gate = jax.nn.sigmoid(gate_pre)
    silu_gate = gate_pre * sigmoid_gate
    hidden = (silu_gate * up_pre).astype(jnp.bfloat16)
    expert_out = jnp.einsum(
        "abecf,efd->abecd", hidden, w_down, preferred_element_type=jnp.float32
    ).astype(jnp.bfloat16)
    return (gate_pre, up_pre, sigmoid_gate, silu_gate, hidden, expert_out)


def expert_backward(tok_in, scaled_in, saved, w_gate, w_up, w_down):
    gate_pre, up_pre, sigmoid_gate, silu_gate, hidden = saved
    hidden_grad = jnp.einsum(
        "abecd,efd->abecf", scaled_in, w_down, preferred_element_type=jnp.float32
    )
    gate_grad = (
        hidden_grad * up_pre * sigmoid_gate * (1.0 + gate_pre * (1.0 - sigmoid_gate))
    ).astype(jnp.bfloat16)
    up_grad = (hidden_grad * silu_gate).astype(jnp.bfloat16)
    pair_grad = (
        jnp.einsum("abecf,edf->abecd", gate_grad, w_gate, preferred_element_type=jnp.float32)
        + jnp.einsum("abecf,edf->abecd", up_grad, w_up, preferred_element_type=jnp.float32)
    ).astype(jnp.bfloat16)
    grad_gate = jnp.einsum(
        "abecd,abecf->edf", tok_in, gate_grad, preferred_element_type=jnp.float32
    )
    grad_up = jnp.einsum("abecd,abecf->edf", tok_in, up_grad, preferred_element_type=jnp.float32)
    grad_down = jnp.einsum(
        "abecf,abecd->efd", hidden, scaled_in, preferred_element_type=jnp.float32
    )
    return (pair_grad, grad_gate, grad_up, grad_down)


def per_device(tokens, cotangent, routes, gate_weights, w_gate, w_up, w_down):
    outer_count = lax.axis_size("outer")
    inner_count = lax.axis_size("inner")
    tok_rows, model_width = tokens.shape
    route_share = routes.shape[1]
    exp_dev = w_gate.shape[0]
    experts = exp_dev * outer_count * inner_count
    pair_count = tok_rows * route_share
    capacity = max(2, 2 * pair_count // experts)
    slot_total = experts * capacity
    flat_ids = routes.reshape(pair_count)
    positions = jnp.arange(pair_count, dtype=jnp.int32)
    earlier = (flat_ids[:, None] == flat_ids[None, :]) & (positions[:, None] > positions[None, :])
    slot_rank = jnp.sum(earlier, axis=1, dtype=jnp.int32)
    slot_index = flat_ids * capacity + slot_rank
    selector = (slot_index[None, :] == jnp.arange(slot_total, dtype=jnp.int32)[:, None]).astype(
        jnp.bfloat16
    )
    gate_flat = gate_weights.reshape(pair_count)
    tok_pairs = jnp.repeat(tokens, route_share, axis=0)
    scaled_pairs = (
        gate_flat[:, None] * jnp.repeat(cotangent, route_share, axis=0).astype(jnp.float32)
    ).astype(jnp.bfloat16)
    slot_shape = (outer_count, inner_count, exp_dev, capacity, model_width)
    tok_slots = (
        jnp.dot(selector, tok_pairs, preferred_element_type=jnp.float32)
        .astype(jnp.bfloat16)
        .reshape(slot_shape)
    )
    scaled_slots = (
        jnp.dot(selector, scaled_pairs, preferred_element_type=jnp.float32)
        .astype(jnp.bfloat16)
        .reshape(slot_shape)
    )
    tok_in, scaled_in = send_rows((tok_slots, scaled_slots))
    forward_vals = expert_forward(tok_in, w_gate, w_up, w_down)
    expert_out = forward_vals[5]
    out_back = return_rows(expert_out)
    pair_grad, grad_gate, grad_up, grad_down = expert_backward(
        tok_in, scaled_in, forward_vals[:5], w_gate, w_up, w_down
    )
    grad_back = return_rows(pair_grad)
    picked = jnp.take(out_back.reshape(slot_total, model_width), slot_index, axis=0)
    picked = picked.reshape(tok_rows, route_share, model_width).astype(jnp.float32)
    picked_grad = jnp.take(grad_back.reshape(slot_total, model_width), slot_index, axis=0)
    picked_grad = picked_grad.reshape(tok_rows, route_share, model_width).astype(jnp.float32)
    combined_part = jnp.sum(gate_weights[:, :, None] * picked, axis=1)
    grad_part = jnp.sum(picked_grad, axis=1)
    token_totals = (
        lax.psum_scatter(
            combined_part.astype(jnp.bfloat16), "rep", scatter_dimension=1, tiled=True
        ).astype(jnp.float32),
        lax.psum_scatter(
            grad_part.astype(jnp.bfloat16), "rep", scatter_dimension=1, tiled=True
        ).astype(jnp.float32),
    )
    summed = (
        lax.psum_scatter(
            grad_gate.astype(jnp.bfloat16), "rep", scatter_dimension=1, tiled=True
        ).astype(jnp.float32),
        lax.psum_scatter(
            grad_up.astype(jnp.bfloat16), "rep", scatter_dimension=1, tiled=True
        ).astype(jnp.float32),
        lax.psum_scatter(
            grad_down.astype(jnp.bfloat16), "rep", scatter_dimension=1, tiled=True
        ).astype(jnp.float32),
    )
    return (
        token_totals[0].astype(jnp.bfloat16),
        token_totals[1].astype(jnp.bfloat16),
        summed[0].astype(jnp.bfloat16),
        summed[1].astype(jnp.bfloat16),
        summed[2].astype(jnp.bfloat16),
    )


def solution(mesh):
    in_specs = (
        P(("outer", "inner"), None),
        P(("outer", "inner"), None),
        P(("outer", "inner"), "rep"),
        P(("outer", "inner"), "rep"),
        P(("outer", "inner"), None, None),
        P(("outer", "inner"), None, None),
        P(("outer", "inner"), None, None),
    )
    out_specs = (
        P(("outer", "inner"), "rep"),
        P(("outer", "inner"), "rep"),
        P(("outer", "inner"), "rep", None),
        P(("outer", "inner"), "rep", None),
        P(("outer", "inner"), "rep", None),
    )
    return jax.shard_map(
        per_device, mesh=mesh, in_specs=in_specs, out_specs=out_specs, check_vma=False
    )
```

profile of v0, /device:TPU:1, one launch (start us, length us, event | category | flops | bytes accessed | tf_op | source)
XLA Modules:
  0.0 455.5 jit_solution(7143746801339264389)
XLA Ops:
  7.2 0.9 convert_reduce_fusion
  8.1 0.7 compare_and_fusion
  8.8 1.3 convolution_convert_fusion.1
  10.1 0.2 reshape.108
  10.3 0.9 copy.48
  11.3 19.4 %all-to-all-start.4 = ((bf16[16,8,1,2,1024]{4,1,3,2,0:T(8,128)(2,1)}), bf16[16,8,1,2,1024]{4,1,3,2,0:T(8,128)(2,1)S(1)}, u32[]{:S(2)}, u32[]{:S(2)}) async-start(bf16[16,8,1,2,1024]{4,1,3,2,0:T(8,128)(2,1)} %copy.48), calls=%async_computation.4 | async-start | bytes 1048576 | tf_op jit(solution)/shard_map/all_to_all | solution.py:17
  30.7 0.3 convolution_convert_fusion.2
  31.0 0.2 reshape.101
  31.2 0.9 copy.42
  32.1 21.4 %all-to-all-done.4 = bf16[16,8,1,2,1024]{4,1,3,2,0:T(8,128)(2,1)S(1)} async-done(((bf16[16,8,1,2,1024]{4,1,3,2,0:T(8,128)(2,1)}), bf16[16,8,1,2,1024]{4,1,3,2,0:T(8,128)(2,1)S(1)}, u32[]{:S(2)}, u32[]{:S(2)}) %all-to-all-start.4) | async-done | bytes 524320 | tf_op jit(solution)/shard_map/all_to_all | solution.py:17
  53.5 12.5 %all-to-all-start = ((bf16[16,8,1,2,1024]{4,1,3,2,0:T(8,128)(2,1)}), bf16[16,8,1,2,1024]{4,1,3,2,0:T(8,128)(2,1)S(1)}, u32[]{:S(2)}, u32[]{:S(2)}) async-start(bf16[16,8,1,2,1024]{4,1,3,2,0:T(8,128)(2,1)} %copy.42), calls=%async_computation | async-start | bytes 1048576 | tf_op jit(solution)/shard_map/all_to_all | solution.py:10
  66.1 1.4 copy.49
  67.4 21.5 %all-to-all-done = bf16[16,8,1,2,1024]{4,1,3,2,0:T(8,128)(2,1)S(1)} async-done(((bf16[16,8,1,2,1024]{4,1,3,2,0:T(8,128)(2,1)}), bf16[16,8,1,2,1024]{4,1,3,2,0:T(8,128)(2,1)S(1)}, u32[]{:S(2)}, u32[]{:S(2)}) %all-to-all-start) | async-done | bytes 524320 | tf_op jit(solution)/shard_map/all_to_all | solution.py:10
  88.9 11.6 %all-to-all-start.5 = ((bf16[16,8,1,2,1024]{4,3,0,2,1:T(2,128)(2,1)}), bf16[16,8,1,2,1024]{4,3,0,2,1:T(2,128)(2,1)S(1)}, u32[]{:S(2)}, u32[]{:S(2)}) async-start(bf16[16,8,1,2,1024]{4,3,0,2,1:T(2,128)(2,1)} %copy.49), calls=%async_computation.5 | async-start | bytes 1048576 | tf_op jit(solution)/shard_map/all_to_all | solution.py:16
  100.4 1.3 copy.43
  101.8 8.1 %all-to-all-done.5 = bf16[16,8,1,2,1024]{4,3,0,2,1:T(2,128)(2,1)S(1)} async-done(((bf16[16,8,1,2,1024]{4,3,0,2,1:T(2,128)(2,1)}), bf16[16,8,1,2,1024]{4,3,0,2,1:T(2,128)(2,1)S(1)}, u32[]{:S(2)}, u32[]{:S(2)}) %all-to-all-start.5) | async-done | bytes 524320 | tf_op jit(solution)/shard_map/all_to_all | solution.py:16
  109.9 4.3 all-to-all-start.1
  114.2 1.3 convolution_bitcast_fusion
  115.5 8.2 %all-to-all-done.1 = bf16[16,8,1,2,1024]{4,3,0,2,1:T(2,128)(2,1)S(1)} async-done(((bf16[16,8,1,2,1024]{4,3,0,2,1:T(2,128)(2,1)}), bf16[16,8,1,2,1024]{4,3,0,2,1:T(2,128)(2,1)S(1)}, u32[]{:S(2)}, u32[]{:S(2)}) %all-to-all-start.1) | async-done | bytes 524320 | tf_op jit(solution)/shard_map/all_to_all | solution.py:9
  123.7 0.5 convolution_bitcast_fusion.1
  124.2 0.5 copy-done.3
  124.7 1.4 fusion.28
  126.0 0.7 copy-done.7
  126.7 1.3 fusion.5
  128.0 6.1 %all-to-all-start.2 = ((bf16[16,8,1,2,1024]{4,1,3,2,0:T(8,128)(2,1)}), bf16[16,8,1,2,1024]{4,1,3,2,0:T(8,128)(2,1)S(1)}, u32[]{:S(2)}, u32[]{:S(2)}) async-start(bf16[16,8,1,2,1024]{4,1,3,2,0:T(8,128)(2,1)} %fusion.5), calls=%async_computation.2 | async-start | bytes 1048576 | tf_op jit(solution)/shard_map/all_to_all | solution.py:28
  134.2 0.5 fusion.8
  134.7 0.4 copy-done.5
  135.1 1.3 fusion.4
  136.4 20.7 %all-to-all-done.2 = bf16[16,8,1,2,1024]{4,1,3,2,0:T(8,128)(2,1)S(1)} async-done(((bf16[16,8,1,2,1024]{4,1,3,2,0:T(8,128)(2,1)}), bf16[16,8,1,2,1024]{4,1,3,2,0:T(8,128)(2,1)S(1)}, u32[]{:S(2)}, u32[]{:S(2)}) %all-to-all-start.2) | async-done | bytes 524320 | tf_op jit(solution)/shard_map/all_to_all | solution.py:28
  157.1 12.2 %all-to-all-start.6 = ((bf16[16,8,1,2,1024]{4,1,3,2,0:T(8,128)(2,1)}), bf16[16,8,1,2,1024]{4,1,3,2,0:T(8,128)(2,1)S(1)}, u32[]{:S(2)}, u32[]{:S(2)}) async-start(bf16[16,8,1,2,1024]{4,1,3,2,0:T(8,128)(2,1)} %fusion.4), calls=%async_computation.6 | async-start | bytes 1048576 | tf_op jit(solution)/shard_map/all_to_all | solution.py:28
  169.2 1.3 copy.46
  170.6 21.5 %all-to-all-done.6 = bf16[16,8,1,2,1024]{4,1,3,2,0:T(8,128)(2,1)S(1)} async-done(((bf16[16,8,1,2,1024]{4,1,3,2,0:T(8,128)(2,1)}), bf16[16,8,1,2,1024]{4,1,3,2,0:T(8,128)(2,1)S(1)}, u32[]{:S(2)}, u32[]{:S(2)}) %all-to-all-start.6) | async-done | bytes 524320 | tf_op jit(solution)/shard_map/all_to_all | solution.py:28
  192.0 10.5 %all-to-all-start.3 = ((bf16[16,8,1,2,1024]{4,3,0,2,1:T(2,128)(2,1)}), bf16[16,8,1,2,1024]{4,3,0,2,1:T(2,128)(2,1)S(1)}, u32[]{:S(2)}, u32[]{:S(2)}) async-start(bf16[16,8,1,2,1024]{4,3,0,2,1:T(2,128)(2,1)} %copy.46), calls=%async_computation.3 | async-start | bytes 1048576 | tf_op jit(solution)/shard_map/all_to_all | solution.py:27
  202.5 1.4 copy.52
  203.9 8.1 %all-to-all-done.3 = bf16[16,8,1,2,1024]{4,3,0,2,1:T(2,128)(2,1)S(1)} async-done(((bf16[16,8,1,2,1024]{4,3,0,2,1:T(2,128)(2,1)}), bf16[16,8,1,2,1024]{4,3,0,2,1:T(2,128)(2,1)S(1)}, u32[]{:S(2)}, u32[]{:S(2)}) %all-to-all-start.3) | async-done | bytes 524320 | tf_op jit(solution)/shard_map/all_to_all | solution.py:27
  212.0 4.3 all-to-all-start.7
  216.3 0.5 copy.47
  216.8 0.2 reshape.107
  217.0 0.9 gather_fusion
  217.9 0.2 multiply_convert_fusion.1
  218.0 0.8 copy.60
  218.9 0.0 reduce-scatter.16.cloned.1.call-update
  218.9 0.0 reduce-scatter.18.cloned.1.call-start
  218.9 6.8 %all-to-all-done.7 = bf16[16,8,1,2,1024]{4,3,0,2,1:T(2,128)(2,1)S(1)} async-done(((bf16[16,8,1,2,1024]{4,3,0,2,1:T(2,128)(2,1)}), bf16[16,8,1,2,1024]{4,3,0,2,1:T(2,128)(2,1)S(1)}, u32[]{:S(2)}, u32[]{:S(2)}) %all-to-all-start.7) | async-done | bytes 524320 | tf_op jit(solution)/shard_map/all_to_all | solution.py:27
  225.8 0.5 copy.53
  226.3 0.2 reshape.112
  226.5 0.9 gather_fusion.1
  227.3 0.1 broadcast_select_fusion
  227.4 0.9 copy.62
  228.3 0.0 reduce-scatter.18.cloned.1.call-update
  228.3 0.0 reduce-scatter.14.cloned.1.call-start
  228.4 1.4 fusion.3
  229.8 0.0 reduce-scatter.14.cloned.1.call-update
  229.9 0.0 reduce-scatter.12.cloned.1.call-start
  229.9 1.5 fusion.2
  231.4 0.0 reduce-scatter.10.cloned.1.call-start
  231.5 1.4 fusion.1
  233.0 21.6 %reduce-scatter.16.cloned.1.call-done = bf16[128,128]{1,0:T(8,128)(2,1)} async-done(((bf16[1024,128]{1,0:T(8,128)(2,1)}), bf16[128,128]{1,0:T(8,128)(2,1)}) %reduce-scatter.16.cloned.1.call-update) | async-done | bytes 32784
  254.6 1.5 copy.61
  256.0 46.0 %reduce-scatter.18.cloned.1.call-done = bf16[128,128]{1,0:T(8,128)(2,1)} async-done(((bf16[1024,128]{1,0:T(8,128)(2,1)}), bf16[128,128]{1,0:T(8,128)(2,1)}) %reduce-scatter.18.cloned.1.call-update) | async-done | bytes 32784
  302.0 1.5 copy.63
  303.5 47.8 %reduce-scatter.14.cloned.1.call-done = bf16[1,48,1024]{2,1,0:T(8,128)(2,1)} async-done(((bf16[1,384,1024]{2,1,0:T(8,128)(2,1)}), bf16[1,48,1024]{2,1,0:T(8,128)(2,1)}) %reduce-scatter.14.cloned.1.call-update) | async-done | bytes 98320 | tf_op jit(solution)/shard_map/reduce_scatter | solution.py:134
  351.3 49.0 %reduce-scatter.12.cloned.1.call-done = bf16[1,128,384]{2,1,0:T(8,128)(2,1)} async-done(((bf16[1,1024,384]{2,1,0:T(8,128)(2,1)}), bf16[1,128,384]{2,1,0:T(8,128)(2,1)}) %reduce-scatter.12.cloned.1.call-update) | async-done | bytes 98320 | tf_op jit(solution)/shard_map/reduce_scatter | solution.py:131
  400.3 48.6 %reduce-scatter.10.cloned.1.call-done = bf16[1,128,384]{2,1,0:T(8,128)(2,1)} async-done(((bf16[1,1024,384]{2,1,0:T(8,128)(2,1)}), bf16[1,128,384]{2,1,0:T(8,128)(2,1)}) %reduce-scatter.10.cloned.1.call-update) | async-done | bytes 98320 | tf_op jit(solution)/shard_map/reduce_scatter | solution.py:128
  (26 shorter events, 0.1 us)
Async XLA Ops:
  7.2 117.0 %copy-start = (bf16[1,1024,384]{2,1,0:T(8,128)(2,1)S(1)}, bf16[1,1024,384]{2,1,0:T(8,128)(2,1)}, u32[]{:S(2)}) copy-start(bf16[1,1024,384]{2,1,0:T(8,128)(2,1)} %param.13) | copy-start | bytes 2359300
  10.3 20.4 %copy-start.4 = (bf16[128,1024]{1,0:T(8,128)(2,1)S(1)}, bf16[128,1024]{1,0:T(8,128)(2,1)}, u32[]{:S(2)}) copy-start(bf16[128,1024]{1,0:T(8,128)(2,1)} %param.9) | copy-start | bytes 786436
  11.3 42.3 %all-to-all-start.4 = ((bf16[16,8,1,2,1024]{4,1,3,2,0:T(8,128)(2,1)}), bf16[16,8,1,2,1024]{4,1,3,2,0:T(8,128)(2,1)S(1)}, u32[]{:S(2)}, u32[]{:S(2)}) async-start(bf16[16,8,1,2,1024]{4,1,3,2,0:T(8,128)(2,1)} %copy.48), calls=%async_computation.4 | async-start | bytes 1048576 | tf_op jit(solution)/shard_map/all_to_all | solution.py:17
  53.5 35.4 %all-to-all-start = ((bf16[16,8,1,2,1024]{4,1,3,2,0:T(8,128)(2,1)}), bf16[16,8,1,2,1024]{4,1,3,2,0:T(8,128)(2,1)S(1)}, u32[]{:S(2)}, u32[]{:S(2)}) async-start(bf16[16,8,1,2,1024]{4,1,3,2,0:T(8,128)(2,1)} %copy.42), calls=%async_computation | async-start | bytes 1048576 | tf_op jit(solution)/shard_map/all_to_all | solution.py:10
  88.9 21.0 %all-to-all-start.5 = ((bf16[16,8,1,2,1024]{4,3,0,2,1:T(2,128)(2,1)}), bf16[16,8,1,2,1024]{4,3,0,2,1:T(2,128)(2,1)S(1)}, u32[]{:S(2)}, u32[]{:S(2)}) async-start(bf16[16,8,1,2,1024]{4,3,0,2,1:T(2,128)(2,1)} %copy.49), calls=%async_computation.5 | async-start | bytes 1048576 | tf_op jit(solution)/shard_map/all_to_all | solution.py:16
  100.4 13.8 %copy-start.1 = (bf16[1,384,1024]{2,1,0:T(8,128)(2,1)S(1)}, bf16[1,384,1024]{2,1,0:T(8,128)(2,1)}, u32[]{:S(2)}) copy-start(bf16[1,384,1024]{2,1,0:T(8,128)(2,1)} %param.15) | copy-start | bytes 2359300
  109.9 13.8 %all-to-all-start.1 = ((bf16[16,8,1,2,1024]{4,3,0,2,1:T(2,128)(2,1)}), bf16[16,8,1,2,1024]{4,3,0,2,1:T(2,128)(2,1)S(1)}, u32[]{:S(2)}, u32[]{:S(2)}) async-start(bf16[16,8,1,2,1024]{4,3,0,2,1:T(2,128)(2,1)} %copy.43), calls=%async_computation.1 | async-start | bytes 1048576 | tf_op jit(solution)/shard_map/all_to_all | solution.py:9
  114.2 9.5 %copy-start.2 = (bf16[1,1024,384]{2,1,0:T(8,128)(2,1)S(1)}, bf16[1,1024,384]{2,1,0:T(8,128)(2,1)}, u32[]{:S(2)}) copy-start(bf16[1,1024,384]{2,1,0:T(8,128)(2,1)} %param.14) | copy-start | bytes 2359300
  123.7 1.0 copy-start.3
  126.0 0.7 copy-start.7
  128.0 6.2 %copy-start.9 = (bf16[16,8,1,2,384]{4,1,3,0,2:T(8,128)(2,1)S(1)}, bf16[16,8,1,2,384]{4,1,3,0,2:T(8,128)(2,1)}, u32[]{:S(2)}) copy-start(bf16[16,8,1,2,384]{4,1,3,0,2:T(8,128)(2,1)} %get-tuple-element.9) | copy-start | bytes 589828
  128.0 29.1 %all-to-all-start.2 = ((bf16[16,8,1,2,1024]{4,1,3,2,0:T(8,128)(2,1)}), bf16[16,8,1,2,1024]{4,1,3,2,0:T(8,128)(2,1)S(1)}, u32[]{:S(2)}, u32[]{:S(2)}) async-start(bf16[16,8,1,2,1024]{4,1,3,2,0:T(8,128)(2,1)} %fusion.5), calls=%async_computation.2 | async-start | bytes 1048576 | tf_op jit(solution)/shard_map/all_to_all | solution.py:28
  134.2 0.9 copy-start.5
  157.1 35.0 %all-to-all-start.6 = ((bf16[16,8,1,2,1024]{4,1,3,2,0:T(8,128)(2,1)}), bf16[16,8,1,2,1024]{4,1,3,2,0:T(8,128)(2,1)S(1)}, u32[]{:S(2)}, u32[]{:S(2)}) async-start(bf16[16,8,1,2,1024]{4,1,3,2,0:T(8,128)(2,1)} %fusion.4), calls=%async_computation.6 | async-start | bytes 1048576 | tf_op jit(solution)/shard_map/all_to_all | solution.py:28
  192.0 20.0 %all-to-all-start.3 = ((bf16[16,8,1,2,1024]{4,3,0,2,1:T(2,128)(2,1)}), bf16[16,8,1,2,1024]{4,3,0,2,1:T(2,128)(2,1)S(1)}, u32[]{:S(2)}, u32[]{:S(2)}) async-start(bf16[16,8,1,2,1024]{4,3,0,2,1:T(2,128)(2,1)} %copy.46), calls=%async_computation.3 | async-start | bytes 1048576 | tf_op jit(solution)/shard_map/all_to_all | solution.py:27
  212.0 13.8 %all-to-all-start.7 = ((bf16[16,8,1,2,1024]{4,3,0,2,1:T(2,128)(2,1)}), bf16[16,8,1,2,1024]{4,3,0,2,1:T(2,128)(2,1)S(1)}, u32[]{:S(2)}, u32[]{:S(2)}) async-start(bf16[16,8,1,2,1024]{4,3,0,2,1:T(2,128)(2,1)} %copy.52), calls=%async_computation.7 | async-start | bytes 1048576 | tf_op jit(solution)/shard_map/all_to_all | solution.py:27
  216.3 38.3 %reduce-scatter.16.cloned.1.call-start = ((), (), s32[]{:S(2)}) async-start(), calls=%async_computation.16 | async-start | bytes 294912
  217.0 0.9 copy-start.11
  218.9 83.1 %reduce-scatter.18.cloned.1.call-start = ((), (), s32[]{:S(2)}) async-start(), calls=%async_computation.17 | async-start | bytes 294912
  227.3 1.1 copy-start.8
  228.3 1.6 copy-start.6
  228.3 122.9 %reduce-scatter.14.cloned.1.call-start = ((), (), s32[]{:S(2)}) async-start(), calls=%async_computation.15 | async-start | bytes 884736 | tf_op jit(solution)/shard_map/reduce_scatter | solution.py:134
  229.9 1.6 copy-start.10
  229.9 170.4 %reduce-scatter.12.cloned.1.call-start = ((), (), s32[]{:S(2)}) async-start(), calls=%async_computation.14 | async-start | bytes 884736 | tf_op jit(solution)/shard_map/reduce_scatter | solution.py:131
  231.4 217.5 %reduce-scatter.10.cloned.1.call-start = ((), (), s32[]{:S(2)}) async-start(), calls=%async_computation.13 | async-start | bytes 884736 | tf_op jit(solution)/shard_map/reduce_scatter | solution.py:128
Sparse Core Ops, SparseCore 0:
  220.5 34.0 reduce-scatter.15
  258.3 43.6 reduce-scatter.17
  306.0 45.2 reduce-scatter.13
  355.5 44.7 reduce-scatter.11
  404.1 44.7 reduce-scatter.9
where the time goes:
time: 461 us; the launch traced here: 455 us
  waiting for transfers between devices  329 us (71%)
  starting transfers between devices  81 us (18%)
  local copies, waits for them, and re-layouts  17.1 us (4%)
  between operations  14 us (3%)
  matrix products  12.1 us (3%)
    unnamed x7, waiting for transfers between devices  67.6 us
    reduce_scatter x1, waiting for transfers between devices, per_device(): lax.psum_scatter(grad_up.astype(jnp.bfloat16), 'rep', scatter_dimension=1...  49 us
    reduce_scatter x1, waiting for transfers between devices, per_device(): lax.psum_scatter(grad_gate.astype(jnp.bfloat16), 'rep', scatter_dimension...  48.6 us
    reduce_scatter x1, waiting for transfers between devices, per_device(): lax.psum_scatter(grad_down.astype(jnp.bfloat16), 'rep', scatter_dimension...  47.8 us
    all_to_all x2, waiting for transfers between devices, return_rows(): lax.all_to_all(arrays_in, 'outer', split_axis=0, concat_axis=0, tiled=True)  42.2 us
    all_to_all x1, waiting for transfers between devices, send_rows(): lax.all_to_all(arrays_in[0], 'outer', split_axis=0, concat_axis=0, tiled=...  21.5 us
    all_to_all x1, waiting for transfers between devices, send_rows(): lax.all_to_all(arrays_in[1], 'outer', split_axis=0, concat_axis=0, tiled=...  21.4 us
    all_to_all x1, starting transfers between devices, send_rows(): lax.all_to_all(arrays_in[1], 'outer', split_axis=0, concat_axis=0, tiled=...  19.4 us
  transfers between devices with their start and end apart: 13, of which 13 were waited for; matrix products, arithmetic and copies ran while one was open for 5% of the time, Pallas kernels for 0%

commit v1 on v0

v1 whole, which is shorter than its diff:
```python
import functools

import jax
import jax.numpy as jnp
from jax import lax
from jax.experimental import pallas as pl
from jax.experimental.pallas import tpu as pltpu
from jax.sharding import PartitionSpec as P

MESH = pl.DeviceIdType.MESH
LANES = 128
F32 = jnp.float32
BF16 = jnp.bfloat16


def dot(a, b, dims=((1,), (0,))):
    return lax.dot_general(a, b, (dims, ((), ())), preferred_element_type=F32)


def kernel(
    sizes,
    tok_ref, cot_ref, routes_ref, gate_ref, wg_hbm, wu_hbm, wd_hbm,
    comb_ref, gtok_ref, gg_ref, gu_ref, gd_ref,
    wg, wu, wd, wide, send, recv, tok_in, sc_in, gpre, upre, hid, both,
    own_gu, own_dn, got_gu, got_dn, put_gu, put_dn, part, parts_in,
    w_sem, a2a_send, a2a_recv, ch_send, ch_recv, rep_send, rep_recv,
):
    n_rep, n_out, n_in, cap = sizes
    peers = n_out * n_in
    rows, width = tok_ref.shape
    blocks = width // LANES
    slots = peers * cap
    half = n_rep // 2
    r, o, i = lax.axis_index("rep"), lax.axis_index("outer"), lax.axis_index("inner")
    me = o * n_in + i

    barrier = pltpu.get_barrier_semaphore()

    def greet(k, c):
        o2, i2 = lax.rem(o + lax.div(k, n_in), n_out), lax.rem(i + lax.rem(k, n_in), n_in)
        pl.semaphore_signal(barrier, inc=1, device_id=(r, o2, i2), device_id_type=MESH)
        return c

    def greet_rep(k, c):
        pl.semaphore_signal(
            barrier, inc=1, device_id=(lax.rem(r + k, n_rep), o, i), device_id_type=MESH
        )
        return c

    lax.fori_loop(1, peers, greet, 0)
    lax.fori_loop(1, n_rep, greet_rep, 0)

    loads = [
        pltpu.make_async_copy(src, dst, w_sem.at[n])
        for n, (src, dst) in enumerate(((wg_hbm, wg), (wu_hbm, wu), (wd_hbm, wd)))
    ]
    for load in loads:
        load.start()

    ids = routes_ref[...].astype(F32)
    sub = lax.broadcasted_iota(jnp.int32, (rows, rows), 0)
    lane = lax.broadcasted_iota(jnp.int32, (rows, rows), 1)
    ids_row = jnp.sum(jnp.where(sub == lane, ids, 0.0), axis=0, keepdims=True)
    same = ids == ids_row
    rank_col = jnp.sum(jnp.where(same & (sub > lane), 1.0, 0.0), axis=1, keepdims=True)
    rank_row = jnp.sum(jnp.where(same & (sub < lane), 1.0, 0.0), axis=0, keepdims=True)
    slot_col = ids * float(cap) + rank_col
    slot_row = ids_row * float(cap) + rank_row
    place = lax.broadcasted_iota(jnp.int32, (slots, rows), 0).astype(F32)
    to_slots = jnp.where(place == slot_row, 1.0, 0.0).astype(BF16)
    place = lax.broadcasted_iota(jnp.int32, (rows, slots), 1).astype(F32)
    from_slots = jnp.where(place == slot_col, 1.0, 0.0).astype(BF16)
    gates = gate_ref[...]

    def pack(rows_f32, n):
        for c in range(blocks):
            wide[pl.ds(c, slots, stride=blocks), :] = rows_f32[:, c * LANES : (c + 1) * LANES]
        send[n] = wide[...].astype(BF16).reshape(peers, cap * blocks, LANES)
        recv[n, pl.ds(me, 1)] = send[n, pl.ds(me, 1)]

    def exchange(n):
        def one(k, c):
            m, di = lax.div(k, n_in), lax.rem(k, n_in)
            up, odd = lax.div(m + 1, 2), lax.rem(m, 2)
            do = odd * up + (1 - odd) * (n_out - up)
            o2, i2 = lax.rem(o + do, n_out), lax.rem(i + di, n_in)
            pltpu.make_async_remote_copy(
                src_ref=send.at[n, o2 * n_in + i2],
                dst_ref=recv.at[n, me],
                send_sem=a2a_send.at[n],
                recv_sem=a2a_recv.at[n],
                device_id=(r, o2, i2),
                device_id_type=MESH,
            ).start()
            return c

        lax.fori_loop(1, peers, one, 0)

    def arrive(n):
        got = recv.at[n, pl.ds(0, peers - 1)]
        pltpu.make_async_copy(got, got, a2a_recv.at[n]).wait()
        wide[...] = recv[n].reshape(slots * blocks, LANES).astype(F32)

    def block(c):
        return wide[pl.ds(c, slots, stride=blocks), :].astype(BF16)

    def unpack(n, dst):
        arrive(n)
        for c in range(blocks):
            dst[:, c * LANES : (c + 1) * LANES] = block(c)

    pack(dot(to_slots, tok_ref[...]), 0)
    pl.semaphore_wait(barrier, peers - 1 + n_rep - 1)
    exchange(0)
    scaled = (gates * cot_ref[...].astype(F32)).astype(BF16)
    pack(dot(to_slots, scaled), 1)
    exchange(1)

    for load in loads:
        load.wait()
    unpack(0, tok_in)
    gpre[...] = dot(tok_in[...], wg[...])
    upre[...] = dot(tok_in[...], wu[...])
    g = gpre[...]
    hid[...] = (g * jax.nn.sigmoid(g) * upre[...]).astype(BF16)
    pack(dot(hid[...], wd[...]), 2)
    exchange(2)

    unpack(1, sc_in)
    hgrad = dot(sc_in[...], wd[...], ((1,), (1,)))
    g = gpre[...]
    s = jax.nn.sigmoid(g)
    f = g.shape[1]
    both[:, :f] = (hgrad * upre[...] * s * (1.0 + g * (1.0 - s))).astype(BF16)
    both[:, f:] = (hgrad * (g * s)).astype(BF16)
    pack(
        dot(both[:, :f], wg[...], ((1,), (1,))) + dot(both[:, f:], wu[...], ((1,), (1,))), 3
    )
    exchange(3)

    own_gu[...] = dot(tok_in[...], both[...], ((0,), (0,))).astype(BF16).reshape(own_gu.shape)
    own_dn[...] = dot(hid[...], sc_in[...], ((0,), (0,))).astype(BF16).reshape(own_dn.shape)

    pair = ((0, 1, own_gu, got_gu, put_gu), (1, 2, own_dn, got_dn, put_dn))

    def cut(a, side):
        ref = own_gu if a == 0 else own_dn
        if a == 0:
            n = ref.shape[1] // 2
            return (pl.ds(side * n, n), slice(None))
        n = ref.shape[2] // 2
        return (slice(None), pl.ds(side * n, n))

    def hop(a, d, t, src):
        got = pair[a][3]
        dst = got.at[d, t - 1]
        if t == half:
            src, dst = src.at[cut(a, d)], dst.at[cut(a, d)]
        to = lax.rem(r + (1 if d == 0 else n_rep - 1), n_rep)
        return pltpu.make_async_remote_copy(
            src_ref=src,
            dst_ref=dst,
            send_sem=ch_send.at[a, d, t - 1],
            recv_sem=ch_recv.at[a, d, t - 1],
            device_id=(to, o, i),
            device_id_type=MESH,
        )

    def owner(d, t):
        return lax.rem(r + (t if d == 0 else n_rep - t), n_rep)

    hops = {}
    for t in range(half, 0, -1):
        for a, unused, own, got, put in pair:
            for d in range(2):
                j = owner(d, t)
                if t == half:
                    src = own.at[j]
                else:
                    hops[a, d, t + 1].wait_recv()
                    if t + 1 == half:
                        x, y = cut(a, d), cut(a, 1 - d)
                        put[(d, t - 1) + x] = (
                            got[(d, t) + x].astype(F32) + own[(j,) + x].astype(F32)
                        ).astype(BF16)
                        put[(d, t - 1) + y] = own[(j,) + y]
                    else:
                        put[d, t - 1] = (got[d, t].astype(F32) + own[j].astype(F32)).astype(BF16)
                    src = put.at[d, t - 1]
                hops[a, d, t] = hop(a, d, t, src)
                hops[a, d, t].start()
    for a, unused, own, got, put in pair:
        for d in range(2):
            hops[a, d, 1].wait_recv()
        total = own[r].astype(F32) + got[0, 0].astype(F32) + got[1, 0].astype(F32)
        total = total.astype(BF16)
        if a == 0:
            gg_ref[0] = total[:, :f]
            gu_ref[0] = total[:, f:]
        else:
            gd_ref[0] = total

    def share(n, weigh):
        arrive(2 + n)
        for c in range(blocks):
            rows_f32 = dot(from_slots, block(c))
            part[n, c] = (gates * rows_f32 if weigh else rows_f32).astype(BF16)
        parts_in[n, pl.ds(r, 1)] = part[n, pl.ds(r, 1)]

        def one(k, c):
            to = lax.rem(r + k, n_rep)
            pltpu.make_async_remote_copy(
                src_ref=part.at[n, to],
                dst_ref=parts_in.at[n, r],
                send_sem=rep_send.at[n],
                recv_sem=rep_recv.at[n],
                device_id=(to, o, i),
                device_id_type=MESH,
            ).start()
            return c

        lax.fori_loop(1, n_rep, one, 0)

    def collect(n, out):
        got = parts_in.at[n, pl.ds(0, n_rep - 1)]
        pltpu.make_async_copy(got, got, rep_recv.at[n]).wait()
        out[...] = jnp.sum(parts_in[n].astype(F32), axis=0).astype(BF16)

    share(0, True)
    share(1, False)
    collect(0, comb_ref)
    collect(1, gtok_ref)

    for n in range(4):
        sent = send.at[n, pl.ds(0, peers - 1)]
        pltpu.make_async_copy(sent, sent, a2a_send.at[n]).wait()
    for n in range(2):
        sent = part.at[n, pl.ds(0, n_rep - 1)]
        pltpu.make_async_copy(sent, sent, rep_send.at[n]).wait()
    for h in hops.values():
        h.wait_send()


def per_device(tokens, cotangent, routes, gate_weights, w_gate, w_up, w_down):
    n_rep, n_out, n_in = (lax.axis_size(a) for a in ("rep", "outer", "inner"))
    rows, width = tokens.shape
    hidden = w_gate.shape[2]
    peers = n_out * n_in
    cap = max(2, 2 * rows // peers)
    blocks = width // LANES
    slots = peers * cap
    half = n_rep // 2
    own = width // n_rep
    dn = hidden // n_rep
    vmem = pl.BlockSpec(memory_space=pltpu.VMEM)
    hbm = pl.BlockSpec(memory_space=pl.ANY)
    dma = pltpu.SemaphoreType.DMA
    return pl.pallas_call(
        functools.partial(kernel, (n_rep, n_out, n_in, cap)),
        out_shape=(
            jax.ShapeDtypeStruct((rows, own), BF16),
            jax.ShapeDtypeStruct((rows, own), BF16),
            jax.ShapeDtypeStruct((1, own, hidden), BF16),
            jax.ShapeDtypeStruct((1, own, hidden), BF16),
            jax.ShapeDtypeStruct((1, dn, width), BF16),
        ),
        in_specs=[vmem] * 4 + [hbm] * 3,
        out_specs=(vmem,) * 5,
        scratch_shapes=[
            pltpu.VMEM((width, hidden), BF16),
            pltpu.VMEM((width, hidden), BF16),
            pltpu.VMEM((hidden, width), BF16),
            pltpu.VMEM((slots * blocks, LANES), F32),
            pltpu.VMEM((4, peers, cap * blocks, LANES), BF16),
            pltpu.VMEM((4, peers, cap * blocks, LANES), BF16),
            pltpu.VMEM((slots, width), BF16),
            pltpu.VMEM((slots, width), BF16),
            pltpu.VMEM((slots, hidden), F32),
            pltpu.VMEM((slots, hidden), F32),
            pltpu.VMEM((slots, hidden), BF16),
            pltpu.VMEM((slots, 2 * hidden), BF16),
            pltpu.VMEM((n_rep, own, 2 * hidden), BF16),
            pltpu.VMEM((n_rep, dn, width), BF16),
            pltpu.VMEM((2, half, own, 2 * hidden), BF16),
            pltpu.VMEM((2, half, dn, width), BF16),
            pltpu.VMEM((2, half - 1, own, 2 * hidden), BF16),
            pltpu.VMEM((2, half - 1, dn, width), BF16),
            pltpu.VMEM((2, n_rep, rows, own), BF16),
            pltpu.VMEM((2, n_rep, rows, own), BF16),
            dma((3,)), dma((4,)), dma((4,)), dma((2, 2, half)), dma((2, 2, half)),
            dma((2,)), dma((2,)),
        ],
        compiler_params=pltpu.CompilerParams(
            collective_id=0, has_side_effects=True, vmem_limit_bytes=48 * 1024 * 1024
        ),
        cost_estimate=pl.CostEstimate(
            flops=18 * slots * width * hidden, bytes_accessed=8 * width * hidden, transcendentals=0
        ),
    )(
        tokens, cotangent, routes, gate_weights,
        w_gate.reshape(width, hidden), w_up.reshape(width, hidden), w_down.reshape(hidden, width),
    )


def solution(mesh):
    at = ("outer", "inner")
    rows = P(at, None)
    pairs = P(at, "rep")
    weights = P(at, None, None)
    grads = P(at, "rep", None)
    return jax.shard_map(
        per_device,
        mesh=mesh,
        in_specs=(rows, rows, pairs, pairs, weights, weights, weights),
        out_specs=(pairs, pairs, grads, grads, grads),
        check_vma=False,
    )
```

time: 461 us -> 143 us (0.31)
  waiting for transfers between devices: 329 us -> 0 us
  Pallas kernels: 0 us -> 130 us
  starting transfers between devices: 81 us -> 0 us
  between operations: 14 us -> 0.66 us
  matrix products: 12.1 us -> 0 us
  local copies, waits for them, and re-layouts: 17.1 us -> 9.86 us
    reduce_scatter x3 -> x0, waiting for transfers between devices: 145 us -> none  [the longest x1 49 us: per_device(): lax.psum_scatter(grad_up.astype(jnp.bfloat16), 'rep', scatter_dimension=1...]
    pallas_call x0 -> x1, Pallas kernels: none -> 130 us  [per_device(): pl.pallas_call(functools.partial(kernel, (n_rep, n_out, n_in, cap)), out_...]
    all_to_all x8 -> x0, waiting for transfers between devices: 116 us -> none  [the longest x2 42.2 us: return_rows(): lax.all_to_all(arrays_in, 'outer', split_axis=0, concat_axis=0, tiled=True)]
    all_to_all x8 -> x0, starting transfers between devices: 80.8 us -> none  [the longest x1 19.4 us: send_rows(): lax.all_to_all(arrays_in[1], 'outer', split_axis=0, concat_axis=0, tiled=...]
    unnamed x7 -> x0, waiting for transfers between devices: 67.6 us -> none
    dot_general x11 -> x0, matrix products: 12.1 us -> none  [the longest x1 1.48 us: expert_backward(): jnp.einsum('abecd,abecf->edf', tok_in, up_grad, preferred_element_type=jn...]
    all_to_all x6 -> x0, local copies, waits for them, and re-layouts: 6.35 us -> none  [the longest x2 2.7 us: return_rows(): lax.all_to_all(arrays_in, 'outer', split_axis=0, concat_axis=0, tiled=True)]
    unnamed x28 -> x21, local copies, waits for them, and re-layouts: 6.33 us -> 9.86 us
  transfers between devices with their start and end apart: 13 -> 0, of which waited for: 13 -> 0; matrix products, arithmetic and copies ran while one was open for 5% -> 0% of each run, Pallas kernels for 0% -> 0%
where the time goes in v1:
time: 143 us; the launch traced here: 140 us
  Pallas kernels  130 us (91%)
  local copies, waits for them, and re-layouts  9.86 us (7%)
    pallas_call x1, Pallas kernels, per_device(): pl.pallas_call(functools.partial(kernel, (n_rep, n_out, n_in, cap)), out_...  130 us
    unnamed x21, local copies, waits for them, and re-layouts  9.86 us

profile of v1, /device:TPU:1, one launch (start us, length us, event | category | flops | bytes accessed | tf_op | source)
XLA Modules:
  0.0 140.2 jit_solution(15911451563081479302)
XLA Ops:
  0.6 0.0 copy-start.5
  0.6 0.6 copy-done.5
  1.3 0.0 copy-start.6
  1.3 0.1 copy.12.routes_ref
  1.4 0.5 copy-done.6
  1.9 0.1 copy.13.gate_ref
  2.1 0.0 copy-start
  2.1 1.1 copy-done
  3.2 0.0 copy-start.1
  3.2 1.1 copy-done.1
  4.3 0.0 copy-start.2
  4.3 1.1 copy-done.2
  5.5 0.0 copy-start.3
  5.5 0.9 copy-done.3
  6.4 0.0 copy-start.4
  6.4 0.9 copy-done.4
  7.4 129.7 %shard_map.110 = (bf16[128,128]{1,0:T(8,128)(2,1)S(1)}, bf16[128,128]{1,0:T(8,128)(2,1)S(1)}, bf16[1,128,384]{2,1,0:T(8,128)(2,1)S(1)}, bf16[1,128,384]{2,1,0:T(8,128)(2,1)S(1)}, bf16[1,48,1024]{2,1,0:T(8,128)(2,1)S(1)}) custom-call(bf16[128,1024]{1,0:T(8,128)(2,1)S(1)} %copy-done.3, bf16[128,1024]{1,0:T(8,128)(2,1)S(1)} %copy-done.4, ...), custom_call_target="tpu_custom_call" | custom-call | flops 1811939328 | bytes 3145728 | tf_op jit(solution)/shard_map/pallas_call | solution.py:258
  137.1 0.6 copy.19
  137.7 0.6 copy.20
  138.3 0.6 copy.21
  139.0 0.6 copy.22
  139.6 0.6 copy.23
Async XLA Ops:
  0.6 0.7 copy-start.5
  1.3 0.7 copy-start.6
  2.1 1.1 copy-start
  3.2 1.1 copy-start.1
  4.3 1.1 copy-start.2
  5.5 0.9 copy-start.3
  6.4 0.9 copy-start.4

commit v2 on v1

--- a/solution.py
+++ b/solution.py
@@ -19,21 +19,29 @@
 
 def kernel(
     sizes,
-    tok_ref, cot_ref, routes_ref, gate_ref, wg_hbm, wu_hbm, wd_hbm,
+    tok_hbm, cot_hbm, routes_hbm, gate_hbm, wg_hbm, wu_hbm, wd_hbm,
     comb_ref, gtok_ref, gg_ref, gu_ref, gd_ref,
-    wg, wu, wd, wide, send, recv, tok_in, sc_in, gpre, upre, hid, both,
-    own_gu, own_dn, got_gu, got_dn, put_gu, put_dn, part, parts_in,
+    tok, cot, routes, gate, wg, wu, wd, wide, send, recv, tok_in, sc_in, gpre, upre, hid, both,
+    own_gu, own_dn, got_gu, got_dn, put_gu, put_dn, cols_out, cols_in, note, notes, pick,
     w_sem, a2a_send, a2a_recv, ch_send, ch_recv, rep_send, rep_recv,
 ):
     n_rep, n_out, n_in, cap = sizes
     peers = n_out * n_in
-    rows, width = tok_ref.shape
+    rows, width = tok.shape
     blocks = width // LANES
     slots = peers * cap
     half = n_rep // 2
     r, o, i = lax.axis_index("rep"), lax.axis_index("outer"), lax.axis_index("inner")
     me = o * n_in + i
 
+    operands = (
+        (routes_hbm, routes), (tok_hbm, tok), (gate_hbm, gate), (cot_hbm, cot),
+        (wg_hbm, wg), (wu_hbm, wu), (wd_hbm, wd),
+    )
+    loads = [pltpu.make_async_copy(a, b, w_sem.at[n]) for n, (a, b) in enumerate(operands)]
+    for load in loads:
+        load.start()
+
     barrier = pltpu.get_barrier_semaphore()
 
     def greet(k, c):
@@ -50,31 +58,23 @@
     lax.fori_loop(1, peers, greet, 0)
     lax.fori_loop(1, n_rep, greet_rep, 0)
 
-    loads = [
-        pltpu.make_async_copy(src, dst, w_sem.at[n])
-        for n, (src, dst) in enumerate(((wg_hbm, wg), (wu_hbm, wu), (wd_hbm, wd)))
-    ]
-    for load in loads:
-        load.start()
-
-    ids = routes_ref[...].astype(F32)
     sub = lax.broadcasted_iota(jnp.int32, (rows, rows), 0)
     lane = lax.broadcasted_iota(jnp.int32, (rows, rows), 1)
-    ids_row = jnp.sum(jnp.where(sub == lane, ids, 0.0), axis=0, keepdims=True)
-    same = ids == ids_row
-    rank_col = jnp.sum(jnp.where(same & (sub > lane), 1.0, 0.0), axis=1, keepdims=True)
-    rank_row = jnp.sum(jnp.where(same & (sub < lane), 1.0, 0.0), axis=0, keepdims=True)
-    slot_col = ids * float(cap) + rank_col
-    slot_row = ids_row * float(cap) + rank_row
+
+    def column(row):
+        return jnp.sum(jnp.where(sub == lane, row, 0.0), axis=1, keepdims=True)
+
+    loads[0].wait()
+    ids = routes[...].astype(F32)
+    same = column(ids) == ids
+    rank = jnp.sum(jnp.where(same & (sub < lane), 1.0, 0.0), axis=0, keepdims=True)
+    slot = ids * float(cap) + rank
     place = lax.broadcasted_iota(jnp.int32, (slots, rows), 0).astype(F32)
-    to_slots = jnp.where(place == slot_row, 1.0, 0.0).astype(BF16)
-    place = lax.broadcasted_iota(jnp.int32, (rows, slots), 1).astype(F32)
-    from_slots = jnp.where(place == slot_col, 1.0, 0.0).astype(BF16)
-    gates = gate_ref[...]
+    to_slots = jnp.where(place == slot, 1.0, 0.0).astype(BF16)
 
     def pack(rows_f32, n):
         for c in range(blocks):
-            wide[pl.ds(c, slots, stride=blocks), :] = rows_f32[:, c * LANES : (c + 1) * LANES]
+            wide[pl.ds(c, slots, stride=blocks), :] = rows_f32(c)
         send[n] = wide[...].astype(BF16).reshape(peers, cap * blocks, LANES)
         recv[n, pl.ds(me, 1)] = send[n, pl.ds(me, 1)]
 
@@ -109,22 +109,69 @@
         for c in range(blocks):
             dst[:, c * LANES : (c + 1) * LANES] = block(c)
 
-    pack(dot(to_slots, tok_ref[...]), 0)
+    def spread(n, src, dst):
+        def one(k, c):
+            to = lax.rem(r + k, n_rep)
+            pltpu.make_async_remote_copy(
+                src_ref=src(to),
+                dst_ref=dst.at[r],
+                send_sem=rep_send.at[n],
+                recv_sem=rep_recv.at[n],
+                device_id=(to, o, i),
+                device_id_type=MESH,
+            ).start()
+            return c
+
+        lax.fori_loop(1, n_rep, one, 0)
+
+    def spread_done(n, ref, sem):
+        got = ref.at[pl.ds(0, n_rep - 1)]
+        pltpu.make_async_copy(got, got, sem.at[n]).wait()
+
+    def columns_out(n, rows_f32):
+        for c in range(n_rep):
+            cols_out[n, c] = rows_f32[:, c * LANES : (c + 1) * LANES].astype(BF16)
+        cols_in[n, pl.ds(r, 1)] = cols_out[n, pl.ds(r, 1)]
+        spread(n, lambda to: cols_out.at[n, to], cols_in.at[n])
+
+    def columns_back(n):
+        spread_done(n, cols_in.at[n], rep_recv)
+        pack(lambda g: cols_in[n, g].astype(F32), 2 + n)
+        exchange(2 + n)
+
+    def columns_of(value):
+        return lambda c: value[:, c * LANES : (c + 1) * LANES]
+
+    loads[1].wait()
+    pack(columns_of(dot(to_slots, tok[...])), 0)
     pl.semaphore_wait(barrier, peers - 1 + n_rep - 1)
     exchange(0)
-    scaled = (gates * cot_ref[...].astype(F32)).astype(BF16)
-    pack(dot(to_slots, scaled), 1)
+    loads[2].wait()
+    loads[3].wait()
+    scaled = (column(gate[...]) * cot[...].astype(F32)).astype(BF16)
+    pack(columns_of(dot(to_slots, scaled)), 1)
     exchange(1)
 
-    for load in loads:
+    note[...] = jnp.zeros_like(note)
+    note[0:1, :] = slot
+    note[1:2, :] = gate[...]
+    notes[pl.ds(r, 1)] = note[...].reshape((1,) + note.shape)
+    spread(2, lambda to: note, notes)
+
+    for load in loads[4:]:
         load.wait()
     unpack(0, tok_in)
     gpre[...] = dot(tok_in[...], wg[...])
     upre[...] = dot(tok_in[...], wu[...])
     g = gpre[...]
     hid[...] = (g * jax.nn.sigmoid(g) * upre[...]).astype(BF16)
-    pack(dot(hid[...], wd[...]), 2)
-    exchange(2)
+    columns_out(0, dot(hid[...], wd[...]))
+
+    spread_done(2, notes, rep_recv)
+    place_row = lax.broadcasted_iota(jnp.int32, (rows, slots), 1).astype(F32)
+    for n in range(n_rep):
+        pick[n] = jnp.where(place_row == column(notes[n, 0:1, :]), 1.0, 0.0).astype(BF16)
+    columns_back(0)
 
     unpack(1, sc_in)
     hgrad = dot(sc_in[...], wd[...], ((1,), (1,)))
@@ -133,10 +180,9 @@
     f = g.shape[1]
     both[:, :f] = (hgrad * upre[...] * s * (1.0 + g * (1.0 - s))).astype(BF16)
     both[:, f:] = (hgrad * (g * s)).astype(BF16)
-    pack(
-        dot(both[:, :f], wg[...], ((1,), (1,))) + dot(both[:, f:], wu[...], ((1,), (1,))), 3
-    )
-    exchange(3)
+    columns_out(
+        1, dot(both[:, :f], wg[...], ((1,), (1,))) + dot(both[:, f:], wu[...], ((1,), (1,)))
+    )
 
     own_gu[...] = dot(tok_in[...], both[...], ((0,), (0,))).astype(BF16).reshape(own_gu.shape)
     own_dn[...] = dot(hid[...], sc_in[...], ((0,), (0,))).astype(BF16).reshape(own_dn.shape)
@@ -189,6 +235,8 @@
                     src = put.at[d, t - 1]
                 hops[a, d, t] = hop(a, d, t, src)
                 hops[a, d, t].start()
+        if t == half:
+            columns_back(1)
     for a, unused, own, got, put in pair:
         for d in range(2):
             hops[a, d, 1].wait_recv()
@@ -200,45 +248,31 @@
         else:
             gd_ref[0] = total
 
-    def share(n, weigh):
+    def gather(n, weigh, out):
         arrive(2 + n)
-        for c in range(blocks):
-            rows_f32 = dot(from_slots, block(c))
-            part[n, c] = (gates * rows_f32 if weigh else rows_f32).astype(BF16)
-        parts_in[n, pl.ds(r, 1)] = part[n, pl.ds(r, 1)]
-
-        def one(k, c):
-            to = lax.rem(r + k, n_rep)
-            pltpu.make_async_remote_copy(
-                src_ref=part.at[n, to],
-                dst_ref=parts_in.at[n, r],
-                send_sem=rep_send.at[n],
-                recv_sem=rep_recv.at[n],
-                device_id=(to, o, i),
-                device_id_type=MESH,
-            ).start()
-            return c
-
-        lax.fori_loop(1, n_rep, one, 0)
-
-    def collect(n, out):
-        got = parts_in.at[n, pl.ds(0, n_rep - 1)]
-        pltpu.make_async_copy(got, got, rep_recv.at[n]).wait()
-        out[...] = jnp.sum(parts_in[n].astype(F32), axis=0).astype(BF16)
-
-    share(0, True)
-    share(1, False)
-    collect(0, comb_ref)
-    collect(1, gtok_ref)
+        total = jnp.zeros((rows, LANES), F32)
+        for c in range(n_rep):
+            got = dot(pick[c], block(c))
+            total += column(notes[c, 1:2, :]) * got if weigh else got
+        out[...] = total.astype(BF16)
+
+    gather(0, True, comb_ref)
+    gather(1, False, gtok_ref)
 
     for n in range(4):
         sent = send.at[n, pl.ds(0, peers - 1)]
         pltpu.make_async_copy(sent, sent, a2a_send.at[n]).wait()
-    for n in range(2):
-        sent = part.at[n, pl.ds(0, n_rep - 1)]
-        pltpu.make_async_copy(sent, sent, rep_send.at[n]).wait()
+    spread_done(0, cols_out.at[0], rep_send)
+    spread_done(1, cols_out.at[1], rep_send)
+    spread_done(2, notes, rep_send)
     for h in hops.values():
         h.wait_send()
+
+
+def deliver(*refs):
+    n = len(refs) // 2
+    for k in range(n):
+        refs[n + k][...] = refs[k][...]
 
 
 def per_device(tokens, cotangent, routes, gate_weights, w_gate, w_up, w_down):
@@ -255,18 +289,23 @@
     vmem = pl.BlockSpec(memory_space=pltpu.VMEM)
     hbm = pl.BlockSpec(memory_space=pl.ANY)
     dma = pltpu.SemaphoreType.DMA
-    return pl.pallas_call(
+    out_shape = (
+        jax.ShapeDtypeStruct((rows, own), BF16),
+        jax.ShapeDtypeStruct((rows, own), BF16),
+        jax.ShapeDtypeStruct((1, own, hidden), BF16),
+        jax.ShapeDtypeStruct((1, own, hidden), BF16),
+        jax.ShapeDtypeStruct((1, dn, width), BF16),
+    )
+    results = pl.pallas_call(
         functools.partial(kernel, (n_rep, n_out, n_in, cap)),
-        out_shape=(
-            jax.ShapeDtypeStruct((rows, own), BF16),
-            jax.ShapeDtypeStruct((rows, own), BF16),
-            jax.ShapeDtypeStruct((1, own, hidden), BF16),
-            jax.ShapeDtypeStruct((1, own, hidden), BF16),
-            jax.ShapeDtypeStruct((1, dn, width), BF16),
-        ),
-        in_specs=[vmem] * 4 + [hbm] * 3,
+        out_shape=out_shape,
+        in_specs=[hbm] * 7,
         out_specs=(vmem,) * 5,
         scratch_shapes=[
+            pltpu.VMEM((rows, width), BF16),
+            pltpu.VMEM((rows, width), BF16),
+            pltpu.VMEM((1, rows), jnp.int32),
+            pltpu.VMEM((1, rows), F32),
             pltpu.VMEM((width, hidden), BF16),
             pltpu.VMEM((width, hidden), BF16),
             pltpu.VMEM((hidden, width), BF16),
@@ -285,21 +324,30 @@
             pltpu.VMEM((2, half, dn, width), BF16),
             pltpu.VMEM((2, half - 1, own, 2 * hidden), BF16),
             pltpu.VMEM((2, half - 1, dn, width), BF16),
-            pltpu.VMEM((2, n_rep, rows, own), BF16),
-            pltpu.VMEM((2, n_rep, rows, own), BF16),
-            dma((3,)), dma((4,)), dma((4,)), dma((2, 2, half)), dma((2, 2, half)),
-            dma((2,)), dma((2,)),
+            pltpu.VMEM((2, n_rep, slots, LANES), BF16),
+            pltpu.VMEM((2, n_rep, slots, LANES), BF16),
+            pltpu.VMEM((8, rows), F32),
+            pltpu.VMEM((n_rep, 8, rows), F32),
+            pltpu.VMEM((n_rep, rows, slots), BF16),
+            dma((7,)), dma((4,)), dma((4,)), dma((2, 2, half)), dma((2, 2, half)),
+            dma((3,)), dma((3,)),
         ],
         compiler_params=pltpu.CompilerParams(
-            collective_id=0, has_side_effects=True, vmem_limit_bytes=48 * 1024 * 1024
+            collective_id=0, has_side_effects=True, vmem_limit_bytes=60 * 1024 * 1024
         ),
         cost_estimate=pl.CostEstimate(
             flops=18 * slots * width * hidden, bytes_accessed=8 * width * hidden, transcendentals=0
         ),
     )(
-        tokens, cotangent, routes, gate_weights,
+        tokens, cotangent, routes.reshape(1, rows), gate_weights.reshape(1, rows),
         w_gate.reshape(width, hidden), w_up.reshape(width, hidden), w_down.reshape(hidden, width),
     )
+    return pl.pallas_call(
+        deliver,
+        out_shape=out_shape,
+        in_specs=[vmem] * 5,
+        out_specs=(vmem,) * 5,
+    )(*results)
 
 
 def solution(mesh):

time: 143 us -> 126 us (0.88); the launches traced: 140 us -> 126 us
  local copies, waits for them, and re-layouts: 9.86 us -> 0 us
  Pallas kernels: 130 us -> 126 us
    unnamed x21 -> x0, local copies, waits for them, and re-layouts: 9.86 us -> none
    pallas_call x1, Pallas kernels: 130 us -> 124 us  [per_device(): pl.pallas_call(functools.partial(kernel, (n_rep, n_out, n_in, cap)), out_...]
    pallas_call x0 -> x1, Pallas kernels: none -> 1.76 us  [per_device(): pl.pallas_call(deliver, out_shape=out_shape, in_specs=[vmem] * 5, out_spe...]
where the time goes in v2:
time: 126 us
  Pallas kernels  126 us (100%)
    pallas_call x1, Pallas kernels, per_device(): pl.pallas_call(functools.partial(kernel, (n_rep, n_out, n_in, cap)), out_...  124 us

profile of v2, /device:TPU:1, one launch (start us, length us, event | category | flops | bytes accessed | tf_op | source)
XLA Modules:
  0.0 126.2 jit_solution(12045488443550933473)
XLA Ops:
  0.6 123.8 %shard_map.110 = (bf16[128,128]{1,0:T(8,128)(2,1)}, bf16[128,128]{1,0:T(8,128)(2,1)}, bf16[1,128,384]{2,1,0:T(8,128)(2,1)}, bf16[1,128,384]{2,1,0:T(8,128)(2,1)}, bf16[1,48,1024]{2,1,0:T(8,128)(2,1)}) custom-call(bf16[128,1024]{1,0:T(8,128)(2,1)} %tok_hbm.1, bf16[128,1024]{1,0:T(8,128)(2,1)} %cot_hbm.1, s32[1,128]{1,0:T(1,128)} %bitcast.8, ...), custom_call_target="tpu_custom_call" | custom-call | flops 1811939328 | bytes 3145728 | tf_op jit(solution)/shard_map/pallas_call | solution.py:299
  124.4 1.8 %shard_map.111 = (bf16[128,128]{1,0:T(8,128)(2,1)}, bf16[128,128]{1,0:T(8,128)(2,1)}, bf16[1,128,384]{2,1,0:T(8,128)(2,1)}, bf16[1,128,384]{2,1,0:T(8,128)(2,1)}, bf16[1,48,1024]{2,1,0:T(8,128)(2,1)}) custom-call(bf16[128,128]{1,0:T(8,128)(2,1)} %get-tuple-element.10.refs_0_, bf16[128,128]{1,0:T(8,128)(2,1)} %get-tuple-element.11.refs_1_, ...), custom_call_target="tpu_custom_call" | custom-call | tf_op jit(solution)/shard_map/pallas_call | solution.py:345

commit v3 on v2

--- a/solution.py
+++ b/solution.py
@@ -22,7 +22,7 @@
     tok_hbm, cot_hbm, routes_hbm, gate_hbm, wg_hbm, wu_hbm, wd_hbm,
     comb_ref, gtok_ref, gg_ref, gu_ref, gd_ref,
     tok, cot, routes, gate, wg, wu, wd, wide, send, recv, tok_in, sc_in, gpre, upre, hid, both,
-    own_gu, own_dn, got_gu, got_dn, put_gu, put_dn, cols_out, cols_in, note, notes, pick,
+    own_gu, own_dn, got_gu, got_dn, put_gu, put_dn, cols_out, cols_in, note, notes, pick, pick_all,
     w_sem, a2a_send, a2a_recv, ch_send, ch_recv, rep_send, rep_recv,
 ):
     n_rep, n_out, n_in, cap = sizes
@@ -44,19 +44,22 @@
 
     barrier = pltpu.get_barrier_semaphore()
 
-    def greet(k, c):
-        o2, i2 = lax.rem(o + lax.div(k, n_in), n_out), lax.rem(i + lax.rem(k, n_in), n_in)
-        pl.semaphore_signal(barrier, inc=1, device_id=(r, o2, i2), device_id_type=MESH)
+    inners = [i] + [lax.rem(i + k, n_in) for k in range(1, n_in)]
+
+    def hello(r2, o2, i2):
+        pl.semaphore_signal(barrier, inc=1, device_id=(r2, o2, i2), device_id_type=MESH)
+
+    def greet(m, c):
+        o2 = lax.rem(o + m, n_out)
+        for i2 in inners:
+            hello(r, o2, i2)
         return c
 
-    def greet_rep(k, c):
-        pl.semaphore_signal(
-            barrier, inc=1, device_id=(lax.rem(r + k, n_rep), o, i), device_id_type=MESH
-        )
-        return c
-
-    lax.fori_loop(1, peers, greet, 0)
-    lax.fori_loop(1, n_rep, greet_rep, 0)
+    for i2 in inners[1:]:
+        hello(r, o, i2)
+    lax.fori_loop(1, n_out, greet, 0)
+    for k in range(1, n_rep):
+        hello(lax.rem(r + k, n_rep), o, i)
 
     sub = lax.broadcasted_iota(jnp.int32, (rows, rows), 0)
     lane = lax.broadcasted_iota(jnp.int32, (rows, rows), 1)
@@ -79,11 +82,7 @@
         recv[n, pl.ds(me, 1)] = send[n, pl.ds(me, 1)]
 
     def exchange(n):
-        def one(k, c):
-            m, di = lax.div(k, n_in), lax.rem(k, n_in)
-            up, odd = lax.div(m + 1, 2), lax.rem(m, 2)
-            do = odd * up + (1 - odd) * (n_out - up)
-            o2, i2 = lax.rem(o + do, n_out), lax.rem(i + di, n_in)
+        def one(o2, i2):
             pltpu.make_async_remote_copy(
                 src_ref=send.at[n, o2 * n_in + i2],
                 dst_ref=recv.at[n, me],
@@ -92,13 +91,24 @@
                 device_id=(r, o2, i2),
                 device_id_type=MESH,
             ).start()
+
+        def plane(m, c):
+            up, odd = lax.div(m + 1, 2), lax.rem(m, 2)
+            o2 = lax.rem(o + odd * up + (1 - odd) * (n_out - up), n_out)
+            for i2 in inners:
+                one(o2, i2)
             return c
 
-        lax.fori_loop(1, peers, one, 0)
-
-    def arrive(n):
+        for i2 in inners[1:]:
+            one(o, i2)
+        lax.fori_loop(1, n_out, plane, 0)
+
+    def landed(n):
         got = recv.at[n, pl.ds(0, peers - 1)]
         pltpu.make_async_copy(got, got, a2a_recv.at[n]).wait()
+
+    def arrive(n):
+        landed(n)
         wide[...] = recv[n].reshape(slots * blocks, LANES).astype(F32)
 
     def block(c):
@@ -173,16 +183,43 @@
         pick[n] = jnp.where(place_row == column(notes[n, 0:1, :]), 1.0, 0.0).astype(BF16)
     columns_back(0)
 
-    unpack(1, sc_in)
-    hgrad = dot(sc_in[...], wd[...], ((1,), (1,)))
+    table = jnp.concatenate([notes[n, 0:1, :] for n in range(n_rep)], axis=0).astype(BF16)
+    group = lax.broadcasted_iota(jnp.int32, (n_rep, LANES), 0)
+    of_lane = lax.rem(lax.broadcasted_iota(jnp.int32, (n_rep, LANES), 1), n_rep)
+    spread_slots = dot(table, jnp.where(group == of_lane, 1.0, 0.0).astype(BF16), ((0,), (0,)))
+    at_lane = lax.div(lax.broadcasted_iota(jnp.int32, (rows, LANES), 1), n_rep)
+    for n in range(slots * n_rep // LANES):
+        target = (at_lane + n * (LANES // n_rep)).astype(F32)
+        pick_all[:, n * LANES : (n + 1) * LANES] = jnp.where(
+            spread_slots == target, 1.0, 0.0
+        ).astype(BF16)
+
     g = gpre[...]
     s = jax.nn.sigmoid(g)
     f = g.shape[1]
-    both[:, :f] = (hgrad * upre[...] * s * (1.0 + g * (1.0 - s))).astype(BF16)
-    both[:, f:] = (hgrad * (g * s)).astype(BF16)
-    columns_out(
-        1, dot(both[:, :f], wg[...], ((1,), (1,))) + dot(both[:, f:], wu[...], ((1,), (1,)))
-    )
+    gpre[...] = upre[...] * s * (1.0 + g * (1.0 - s))
+    upre[...] = g * s
+    unpack(1, sc_in)
+    hgrad = dot(sc_in[...], wd[...], ((1,), (1,)))
+    both[:, :f] = (hgrad * gpre[...]).astype(BF16)
+    both[:, f:] = (hgrad * upre[...]).astype(BF16)
+    for k in range(1, n_rep + 1):
+        c = lax.rem(r + k, n_rep)
+        at = pl.ds(pl.multiple_of(c * LANES, LANES), LANES)
+        rows_f32 = dot(both[:, :f], wg[at, :], ((1,), (1,)))
+        rows_f32 += dot(both[:, f:], wu[at, :], ((1,), (1,)))
+        if k == n_rep:
+            cols_in[1, pl.ds(c, 1)] = rows_f32.astype(BF16).reshape(1, slots, LANES)
+        else:
+            cols_out[1, pl.ds(c, 1)] = rows_f32.astype(BF16).reshape(1, slots, LANES)
+            pltpu.make_async_remote_copy(
+                src_ref=cols_out.at[1, c],
+                dst_ref=cols_in.at[1, r],
+                send_sem=rep_send.at[1],
+                recv_sem=rep_recv.at[1],
+                device_id=(c, o, i),
+                device_id_type=MESH,
+            ).start()
 
     own_gu[...] = dot(tok_in[...], both[...], ((0,), (0,))).astype(BF16).reshape(own_gu.shape)
     own_dn[...] = dot(hid[...], sc_in[...], ((0,), (0,))).astype(BF16).reshape(own_dn.shape)
@@ -215,6 +252,7 @@
     def owner(d, t):
         return lax.rem(r + (t if d == 0 else n_rep - t), n_rep)
 
+    columns_back(1)
     hops = {}
     for t in range(half, 0, -1):
         for a, unused, own, got, put in pair:
@@ -235,8 +273,6 @@
                     src = put.at[d, t - 1]
                 hops[a, d, t] = hop(a, d, t, src)
                 hops[a, d, t].start()
-        if t == half:
-            columns_back(1)
     for a, unused, own, got, put in pair:
         for d in range(2):
             hops[a, d, 1].wait_recv()
@@ -248,16 +284,13 @@
         else:
             gd_ref[0] = total
 
-    def gather(n, weigh, out):
-        arrive(2 + n)
-        total = jnp.zeros((rows, LANES), F32)
-        for c in range(n_rep):
-            got = dot(pick[c], block(c))
-            total += column(notes[c, 1:2, :]) * got if weigh else got
-        out[...] = total.astype(BF16)
-
-    gather(0, True, comb_ref)
-    gather(1, False, gtok_ref)
+    arrive(2)
+    total = jnp.zeros((rows, LANES), F32)
+    for c in range(n_rep):
+        total += column(notes[c, 1:2, :]) * dot(pick[c], block(c))
+    comb_ref[...] = total.astype(BF16)
+    landed(3)
+    gtok_ref[...] = dot(pick_all[...], recv[3].reshape(slots * n_rep, LANES)).astype(BF16)
 
     for n in range(4):
         sent = send.at[n, pl.ds(0, peers - 1)]
@@ -329,6 +362,7 @@
             pltpu.VMEM((8, rows), F32),
             pltpu.VMEM((n_rep, 8, rows), F32),
             pltpu.VMEM((n_rep, rows, slots), BF16),
+            pltpu.VMEM((rows, slots * n_rep), BF16),
             dma((7,)), dma((4,)), dma((4,)), dma((2, 2, half)), dma((2, 2, half)),
             dma((3,)), dma((3,)),
         ],

time: 126 us -> 126 us (level)
  no operation moved by 1% of the time
where the time goes in v3:
time: 126 us
  Pallas kernels  125 us (99%)
    pallas_call x1, Pallas kernels, per_device(): pl.pallas_call(functools.partial(kernel, (n_rep, n_out, n_in, cap)), out_...  124 us

profile of v3, /device:TPU:1, one launch (start us, length us, event | category | flops | bytes accessed | tf_op | source)
XLA Modules:
  0.0 125.9 jit_solution(4740791064994067604)
XLA Ops:
  0.6 123.5 %shard_map.110 = (bf16[128,128]{1,0:T(8,128)(2,1)}, bf16[128,128]{1,0:T(8,128)(2,1)}, bf16[1,128,384]{2,1,0:T(8,128)(2,1)}, bf16[1,128,384]{2,1,0:T(8,128)(2,1)}, bf16[1,48,1024]{2,1,0:T(8,128)(2,1)}) custom-call(bf16[128,1024]{1,0:T(8,128)(2,1)} %tok_hbm.1, bf16[128,1024]{1,0:T(8,128)(2,1)} %cot_hbm.1, s32[1,128]{1,0:T(1,128)} %bitcast.8, ...), custom_call_target="tpu_custom_call" | custom-call | flops 1811939328 | bytes 3145728 | tf_op jit(solution)/shard_map/pallas_call | solution.py:332
  124.2 1.8 %shard_map.111 = (bf16[128,128]{1,0:T(8,128)(2,1)}, bf16[128,128]{1,0:T(8,128)(2,1)}, bf16[1,128,384]{2,1,0:T(8,128)(2,1)}, bf16[1,128,384]{2,1,0:T(8,128)(2,1)}, bf16[1,48,1024]{2,1,0:T(8,128)(2,1)}) custom-call(bf16[128,128]{1,0:T(8,128)(2,1)} %get-tuple-element.10.refs_0_, bf16[128,128]{1,0:T(8,128)(2,1)} %get-tuple-element.11.refs_1_, ...), custom_call_target="tpu_custom_call" | custom-call | tf_op jit(solution)/shard_map/pallas_call | solution.py:379

commit v4 on v3

--- a/solution.py
+++ b/solution.py
@@ -252,7 +252,6 @@
     def owner(d, t):
         return lax.rem(r + (t if d == 0 else n_rep - t), n_rep)
 
-    columns_back(1)
     hops = {}
     for t in range(half, 0, -1):
         for a, unused, own, got, put in pair:
@@ -273,6 +272,8 @@
                     src = put.at[d, t - 1]
                 hops[a, d, t] = hop(a, d, t, src)
                 hops[a, d, t].start()
+        if t == half:
+            columns_back(1)
     for a, unused, own, got, put in pair:
         for d in range(2):
             hops[a, d, 1].wait_recv()

time: 126 us -> 126 us (level)
  no operation moved by 1% of the time
where the time goes in v4:
time: 126 us
  Pallas kernels  125 us (99%)
    pallas_call x1, Pallas kernels, per_device(): pl.pallas_call(functools.partial(kernel, (n_rep, n_out, n_in, cap)), out_...  123 us

profile of v4, /device:TPU:1, one launch (start us, length us, event | category | flops | bytes accessed | tf_op | source)
XLA Modules:
  0.0 125.8 jit_solution(517045749866066518)
XLA Ops:
  0.6 123.4 %shard_map.110 = (bf16[128,128]{1,0:T(8,128)(2,1)}, bf16[128,128]{1,0:T(8,128)(2,1)}, bf16[1,128,384]{2,1,0:T(8,128)(2,1)}, bf16[1,128,384]{2,1,0:T(8,128)(2,1)}, bf16[1,48,1024]{2,1,0:T(8,128)(2,1)}) custom-call(bf16[128,1024]{1,0:T(8,128)(2,1)} %tok_hbm.1, bf16[128,1024]{1,0:T(8,128)(2,1)} %cot_hbm.1, s32[1,128]{1,0:T(1,128)} %bitcast.8, ...), custom_call_target="tpu_custom_call" | custom-call | flops 1811939328 | bytes 3145728 | tf_op jit(solution)/shard_map/pallas_call | solution.py:333
  124.0 1.8 %shard_map.111 = (bf16[128,128]{1,0:T(8,128)(2,1)}, bf16[128,128]{1,0:T(8,128)(2,1)}, bf16[1,128,384]{2,1,0:T(8,128)(2,1)}, bf16[1,128,384]{2,1,0:T(8,128)(2,1)}, bf16[1,48,1024]{2,1,0:T(8,128)(2,1)}) custom-call(bf16[128,128]{1,0:T(8,128)(2,1)} %get-tuple-element.10.refs_0_, bf16[128,128]{1,0:T(8,128)(2,1)} %get-tuple-element.11.refs_1_, ...), custom_call_target="tpu_custom_call" | custom-call | tf_op jit(solution)/shard_map/pallas_call | solution.py:380
